TPU v7x, 32 devices: a whole 2x2x4 slice. The times are simulated.
32 devices in a mesh: row: 8 (over y, x, core), col: 4 (over z).
Axes of the slice: x: 2, y: 2, z: 4, core: 2. Of those that a mesh axis runs over, the one named last changes fastest.
Arguments:
- x_blocks: bfloat16 [8, 4, 16, 128, 128], P('row', 'col'), may hold values from -0.8984375 to 0.8984375
- x_live: int32 [8, 4, 16], P('row', 'col'), may hold values 0 or 1
- pair_slots: int32 [8, 4, 4, 3, 192], P('row', 'col'), may hold values from 0 to 15
- pair_count: int32 [8, 4, 4], P('row', 'col'), may hold values from 15 to 192, as said below
Outputs:
- gram_blocks: float32 [8, 4, 16, 128, 128], P('row', 'col')
Inputs may be any that keep to these rules, and one draw needn't show every extreme that they name: `pair_count`: live pairs of a tile at a section; some tile has exactly 192 at its first section.
All inputs are finite; a program needn't handle non-finite values. No bound on the sum of `x_live` on one device may be relied on, other than what follows from the above.
Results may differ from a plain program's by a relative error of at most 0.0003.
Values may be sent and summed in bfloat16 or wider, within the bound.
No kernel may reach another device: no remote copies, remote signals or barrier semaphores. Data moves between devices by JAX's collectives and lax.ppermute only.
A program may use at most 64 MiB of HBM per device.

v0:
```python
import jax
import jax.numpy as jnp
from jax import lax
from jax.sharding import PartitionSpec as P

SECTIONS = 4


def swapped_2(value, axis, distance):
    return lax.ppermute(value, axis, [(i, i ^ 1 << distance) for i in range(lax.axis_size(axis))])


def from_behind(value, axis, by):
    length = lax.axis_size(axis)
    return lax.ppermute(value, axis, [(i, (i + by) % length) for i in range(length)])


def add_pairs(gram_sum, left_piece, right_piece, picked, live_pairs):
    block_size = 48
    block_total = picked.shape[1] // block_size
    slot_total = left_piece.shape[0]
    slot_ids = lax.iota(jnp.int32, slot_total)

    def one_block(block_no, running):
        first_pair = block_no * block_size
        chosen = lax.dynamic_slice_in_dim(picked, first_pair, block_size, 1)
        positions = first_pair + lax.iota(jnp.int32, block_size)
        weights = (positions < live_pairs).astype(jnp.float32)
        left_pick = (chosen[0][:, None] == slot_ids[None, :]).astype(jnp.bfloat16)
        right_pick = (chosen[1][:, None] == slot_ids[None, :]).astype(jnp.bfloat16)
        out_pick = (chosen[2][:, None] == slot_ids[None, :]).astype(jnp.float32) * weights[:, None]
        left_rows = jnp.einsum(
            "ps,sik->pik", left_pick, left_piece, preferred_element_type=jnp.float32
        ).astype(jnp.bfloat16)
        right_rows = jnp.einsum(
            "ps,sjk->pjk", right_pick, right_piece, preferred_element_type=jnp.float32
        ).astype(jnp.bfloat16)
        product = jnp.einsum(
            "pik,pjk->pij", left_rows, right_rows, preferred_element_type=jnp.float32
        )
        added = jnp.einsum("po,pij->oij", out_pick, product, precision=lax.Precision.HIGHEST)
        return running + added

    last_block = jnp.minimum((live_pairs + block_size - 1) // block_size, block_total)
    return lax.fori_loop(0, last_block, one_block, gram_sum)


def body(x_blocks, x_live, pair_slots, pair_count):
    row_total = lax.axis_size("row")
    col_total = lax.axis_size("col")
    layers = row_total // col_total
    col_bits = col_total.bit_length() - 1
    layer_bits = layers.bit_length() - 1
    row_here = lax.axis_index("row")
    col_here = lax.axis_index("col")
    panel_here = row_here // layers
    tile_slots = x_blocks.shape[2]
    block_side = x_blocks.shape[3]
    filtered = x_blocks[0, 0] * x_live[0, 0].astype(jnp.bfloat16)[:, None, None]
    mirrored = filtered
    for bit_no in range(col_bits):
        swapped = swapped_2(mirrored, "row", bit_no + layer_bits)
        swapped = swapped_2(swapped, "col", bit_no)
        differ = panel_here // 2**bit_no % 2 != col_here // 2**bit_no % 2
        mirrored = jnp.where(differ, swapped, mirrored)
    gram_sum = jnp.zeros((tile_slots, block_side, block_side), jnp.float32)
    left_piece = filtered
    right_piece = mirrored
    for section_no in range(SECTIONS):
        if section_no > 0:
            left_piece = from_behind(left_piece, "col", -1)
            right_piece = from_behind(right_piece, "row", -layers)
        gram_sum = add_pairs(
            gram_sum,
            left_piece,
            right_piece,
            pair_slots[0, 0, section_no],
            pair_count[0, 0, section_no],
        )
    return gram_sum[None, None]


def solution(mesh):
    return jax.shard_map(
        body,
        mesh=mesh,
        in_specs=(
            P("row", "col", None, None, None),
            P("row", "col", None),
            P("row", "col", None, None, None),
            P("row", "col", None),
        ),
        out_specs=P("row", "col", None, None, None),
        check_vma=False,
    )
```

profile of v0, /device:TPU:25, one launch (start us, length us, event | category | flops | bytes accessed | tf_op | source)
XLA Modules:
  0.0 215.1 jit_solution(10505156684502976670)
XLA Ops:
  3.1 11.6 %collective-permute-done = bf16[16,128,128]{2,1,0:T(8,128)(2,1)S(1)} collective-permute-done((bf16[16,128,128]{2,1,0:T(8,128)(2,1)S(1)}, bf16[16,128,128]{2,1,0:T(8,128)(2,1)S(1)}, u32[]{:S(2)}, u32[]{:S(2)}) %collective-permute-start) | collective-permute-done | bytes 524320 | tf_op jit(solution)/shard_map/ppermute | solution.py:10
  16.2 10.6 %collective-permute-done.1 = bf16[16,128,128]{2,1,0:T(8,128)(2,1)S(1)} collective-permute-done((bf16[16,128,128]{2,1,0:T(8,128)(2,1)S(1)}, bf16[16,128,128]{2,1,0:T(8,128)(2,1)S(1)}, u32[]{:S(2)}, u32[]{:S(2)}) %collective-permute-start.1) | collective-permute-done | bytes 524320 | tf_op jit(solution)/shard_map/ppermute | solution.py:10
  29.3 8.3 %collective-permute-done.4 = bf16[16,128,128]{2,1,0:T(8,128)(2,1)S(1)} collective-permute-done((bf16[16,128,128]{2,1,0:T(8,128)(2,1)S(1)}, bf16[16,128,128]{2,1,0:T(8,128)(2,1)S(1)}, u32[]{:S(2)}, u32[]{:S(2)}) %collective-permute-start.4) | collective-permute-done | bytes 524320 | tf_op jit(solution)/shard_map/ppermute | solution.py:15
  41.8 5.9 %collective-permute-done.6 = bf16[16,128,128]{2,1,0:T(8,128)(2,1)} collective-permute-done((bf16[16,128,128]{2,1,0:T(8,128)(2,1)S(1)}, bf16[16,128,128]{2,1,0:T(8,128)(2,1)}, u32[]{:S(2)}, u32[]{:S(2)}) %collective-permute-start.6) | collective-permute-done | bytes 524320 | tf_op jit(solution)/shard_map/ppermute | solution.py:15
  47.9 37.9 %collective-permute-done.3 = bf16[16,128,128]{2,1,0:T(8,128)(2,1)S(1)} collective-permute-done((bf16[16,128,128]{2,1,0:T(8,128)(2,1)S(1)}, bf16[16,128,128]{2,1,0:T(8,128)(2,1)S(1)}, u32[]{:S(2)}, u32[]{:S(2)}) %collective-permute-start.3) | collective-permute-done | bytes 524320 | tf_op jit(solution)/shard_map/ppermute | solution.py:10
  89.0 30.8 %while.48 = (s32[]{:T(128)}, f32[16,128,128]{2,0,1:T(8,128)S(1)}, s32[]{:T(128)}, s32[3,192]{1,0:T(4,128)S(1)}, s32[]{:T(128)}, /*index=5*/bf16[16,128,128]{2,1,...) while((s32[]{:T(128)}, f32[16,128,128]{2,0,1:T(8,128)S(1)}, ...), condition=%wide.region_1.2_spmd.clone.clone, body=%wide.region_0.1_spmd.clone.clone.sunk | while | flops 402918528 | bytes 15732071 | solution.py:45
  93.2 3.5 %fusion.147 = f32[16,128,128]{2,0,1:T(8,128)S(1)} fusion(f32[16,128,128]{2,0,1:T(8,128)S(1)} %get-tuple-element.649, f32[48,128,128]{2,1,0:T(8,128)S(1)} %fusion.146, f32[48]{0:T(128)S(1)} %compare_convert_fusion.8, s32[48]{0:T(128)S(1)} %get-tuple-element.606), kind=kOutput, calls=%fused_computation.9.clone.1 | convolution fusion | flops 151258624 | bytes 5243264 | tf_op jit(solution)/shard_map/while/body/po,pij->oij/dot_general | solution.py:41
  100.9 3.5 %fusion.147 = f32[16,128,128]{2,0,1:T(8,128)S(1)} fusion(f32[16,128,128]{2,0,1:T(8,128)S(1)} %get-tuple-element.649, f32[48,128,128]{2,1,0:T(8,128)S(1)} %fusion.146, f32[48]{0:T(128)S(1)} %compare_convert_fusion.8, s32[48]{0:T(128)S(1)} %get-tuple-element.606), kind=kOutput, calls=%fused_computation.9.clone.1 | convolution fusion | flops 151258624 | bytes 5243264 | tf_op jit(solution)/shard_map/while/body/po,pij->oij/dot_general | solution.py:41
  108.6 3.5 %fusion.147 = f32[16,128,128]{2,0,1:T(8,128)S(1)} fusion(f32[16,128,128]{2,0,1:T(8,128)S(1)} %get-tuple-element.649, f32[48,128,128]{2,1,0:T(8,128)S(1)} %fusion.146, f32[48]{0:T(128)S(1)} %compare_convert_fusion.8, s32[48]{0:T(128)S(1)} %get-tuple-element.606), kind=kOutput, calls=%fused_computation.9.clone.1 | convolution fusion | flops 151258624 | bytes 5243264 | tf_op jit(solution)/shard_map/while/body/po,pij->oij/dot_general | solution.py:41
  116.3 3.5 %fusion.147 = f32[16,128,128]{2,0,1:T(8,128)S(1)} fusion(f32[16,128,128]{2,0,1:T(8,128)S(1)} %get-tuple-element.649, f32[48,128,128]{2,1,0:T(8,128)S(1)} %fusion.146, f32[48]{0:T(128)S(1)} %compare_convert_fusion.8, s32[48]{0:T(128)S(1)} %get-tuple-element.606), kind=kOutput, calls=%fused_computation.9.clone.1 | convolution fusion | flops 151258624 | bytes 5243264 | tf_op jit(solution)/shard_map/while/body/po,pij->oij/dot_general | solution.py:41
  120.1 31.3 %while.49 = (s32[]{:T(128)}, f32[16,128,128]{2,0,1:T(8,128)S(1)}, s32[]{:T(128)}, s32[3,192]{1,0:T(4,128)S(1)}, s32[]{:T(128)}, /*index=5*/bf16[16,128,128]{2,1,...) while((s32[]{:T(128)}, f32[16,128,128]{2,0,1:T(8,128)S(1)}, ...), condition=%wide.region_3.4_spmd.clone.clone, body=%wide.region_2.3_spmd.clone.clone.sunk | while | flops 402918528 | bytes 15732071 | solution.py:45
  124.4 3.5 %fusion.157 = f32[16,128,128]{2,0,1:T(8,128)S(1)} fusion(f32[16,128,128]{2,0,1:T(8,128)S(1)} %get-tuple-element.682, f32[48,128,128]{2,1,0:T(8,128)S(1)} %fusion.156, f32[48]{0:T(128)S(1)} %compare_convert_fusion.9, s32[48]{0:T(128)S(1)} %get-tuple-element.616), kind=kOutput, calls=%fused_computation.37.clone.1 | convolution fusion | flops 151258624 | bytes 5243264 | tf_op jit(solution)/shard_map/while/body/po,pij->oij/dot_general | solution.py:41
  132.2 3.5 %fusion.157 = f32[16,128,128]{2,0,1:T(8,128)S(1)} fusion(f32[16,128,128]{2,0,1:T(8,128)S(1)} %get-tuple-element.682, f32[48,128,128]{2,1,0:T(8,128)S(1)} %fusion.156, f32[48]{0:T(128)S(1)} %compare_convert_fusion.9, s32[48]{0:T(128)S(1)} %get-tuple-element.616), kind=kOutput, calls=%fused_computation.37.clone.1 | convolution fusion | flops 151258624 | bytes 5243264 | tf_op jit(solution)/shard_map/while/body/po,pij->oij/dot_general | solution.py:41
  140.0 3.5 %fusion.157 = f32[16,128,128]{2,0,1:T(8,128)S(1)} fusion(f32[16,128,128]{2,0,1:T(8,128)S(1)} %get-tuple-element.682, f32[48,128,128]{2,1,0:T(8,128)S(1)} %fusion.156, f32[48]{0:T(128)S(1)} %compare_convert_fusion.9, s32[48]{0:T(128)S(1)} %get-tuple-element.616), kind=kOutput, calls=%fused_computation.37.clone.1 | convolution fusion | flops 151258624 | bytes 5243264 | tf_op jit(solution)/shard_map/while/body/po,pij->oij/dot_general | solution.py:41
  147.9 3.5 %fusion.157 = f32[16,128,128]{2,0,1:T(8,128)S(1)} fusion(f32[16,128,128]{2,0,1:T(8,128)S(1)} %get-tuple-element.682, f32[48,128,128]{2,1,0:T(8,128)S(1)} %fusion.156, f32[48]{0:T(128)S(1)} %compare_convert_fusion.9, s32[48]{0:T(128)S(1)} %get-tuple-element.616), kind=kOutput, calls=%fused_computation.37.clone.1 | convolution fusion | flops 151258624 | bytes 5243264 | tf_op jit(solution)/shard_map/while/body/po,pij->oij/dot_general | solution.py:41
  151.4 35.2 %while.50 = (s32[]{:T(128)}, f32[16,128,128]{2,0,1:T(8,128)S(1)}, s32[]{:T(128)}, s32[3,192]{1,0:T(4,128)S(1)}, s32[]{:T(128)}, /*index=5*/bf16[16,128,128]{2,1,...) while((s32[]{:T(128)}, f32[16,128,128]{2,0,1:T(8,128)S(1)}, ...), condition=%wide.region_5.6_spmd.clone.clone, body=%wide.region_4.5_spmd.clone.clone.sunk | while | flops 402918528 | bytes 15732071 | solution.py:45
  156.8 3.5 %fusion.167 = f32[16,128,128]{2,0,1:T(8,128)S(1)} fusion(f32[16,128,128]{2,0,1:T(8,128)S(1)} %get-tuple-element.715, f32[48,128,128]{2,1,0:T(8,128)S(1)} %fusion.166, f32[48]{0:T(128)S(1)} %compare_convert_fusion.10, s32[48]{0:T(128)S(1)} %get-tuple-element.626), kind=kOutput, calls=%fused_computation.65.clone.1 | convolution fusion | flops 151258624 | bytes 5243264 | tf_op jit(solution)/shard_map/while/body/po,pij->oij/dot_general | solution.py:41
  165.6 3.5 %fusion.167 = f32[16,128,128]{2,0,1:T(8,128)S(1)} fusion(f32[16,128,128]{2,0,1:T(8,128)S(1)} %get-tuple-element.715, f32[48,128,128]{2,1,0:T(8,128)S(1)} %fusion.166, f32[48]{0:T(128)S(1)} %compare_convert_fusion.10, s32[48]{0:T(128)S(1)} %get-tuple-element.626), kind=kOutput, calls=%fused_computation.65.clone.1 | convolution fusion | flops 151258624 | bytes 5243264 | tf_op jit(solution)/shard_map/while/body/po,pij->oij/dot_general | solution.py:41
  174.4 3.5 %fusion.167 = f32[16,128,128]{2,0,1:T(8,128)S(1)} fusion(f32[16,128,128]{2,0,1:T(8,128)S(1)} %get-tuple-element.715, f32[48,128,128]{2,1,0:T(8,128)S(1)} %fusion.166, f32[48]{0:T(128)S(1)} %compare_convert_fusion.10, s32[48]{0:T(128)S(1)} %get-tuple-element.626), kind=kOutput, calls=%fused_computation.65.clone.1 | convolution fusion | flops 151258624 | bytes 5243264 | tf_op jit(solution)/shard_map/while/body/po,pij->oij/dot_general | solution.py:41
  186.7 27.1 %while.51 = (s32[]{:T(128)}, f32[16,128,128]{2,0,1:T(8,128)S(1)}, s32[]{:T(128)}, s32[3,192]{1,0:T(4,128)S(1)}, s32[]{:T(128)}, /*index=5*/bf16[16,128,128]{2,1,...) while((s32[]{:T(128)}, f32[16,128,128]{2,0,1:T(8,128)S(1)}, ...), condition=%wide.region_7.8_spmd.clone.clone, body=%wide.region_6.7_spmd.clone.clone.sunk | while | flops 402918528 | bytes 15732071 | solution.py:45
  190.2 3.5 %fusion.177 = f32[16,128,128]{2,0,1:T(8,128)S(1)} fusion(f32[16,128,128]{2,0,1:T(8,128)S(1)} %get-tuple-element.748, f32[48,128,128]{2,1,0:T(8,128)S(1)} %fusion.176, f32[48]{0:T(128)S(1)} %compare_convert_fusion.11, s32[48]{0:T(128)S(1)} %get-tuple-element.636), kind=kOutput, calls=%fused_computation.93.clone.1 | convolution fusion | flops 151258624 | bytes 5243264 | tf_op jit(solution)/shard_map/while/body/po,pij->oij/dot_general | solution.py:41
  196.9 3.5 %fusion.177 = f32[16,128,128]{2,0,1:T(8,128)S(1)} fusion(f32[16,128,128]{2,0,1:T(8,128)S(1)} %get-tuple-element.748, f32[48,128,128]{2,1,0:T(8,128)S(1)} %fusion.176, f32[48]{0:T(128)S(1)} %compare_convert_fusion.11, s32[48]{0:T(128)S(1)} %get-tuple-element.636), kind=kOutput, calls=%fused_computation.93.clone.1 | convolution fusion | flops 151258624 | bytes 5243264 | tf_op jit(solution)/shard_map/while/body/po,pij->oij/dot_general | solution.py:41
  203.6 3.5 %fusion.177 = f32[16,128,128]{2,0,1:T(8,128)S(1)} fusion(f32[16,128,128]{2,0,1:T(8,128)S(1)} %get-tuple-element.748, f32[48,128,128]{2,1,0:T(8,128)S(1)} %fusion.176, f32[48]{0:T(128)S(1)} %compare_convert_fusion.11, s32[48]{0:T(128)S(1)} %get-tuple-element.636), kind=kOutput, calls=%fused_computation.93.clone.1 | convolution fusion | flops 151258624 | bytes 5243264 | tf_op jit(solution)/shard_map/while/body/po,pij->oij/dot_general | solution.py:41
  210.3 3.5 %fusion.177 = f32[16,128,128]{2,0,1:T(8,128)S(1)} fusion(f32[16,128,128]{2,0,1:T(8,128)S(1)} %get-tuple-element.748, f32[48,128,128]{2,1,0:T(8,128)S(1)} %fusion.176, f32[48]{0:T(128)S(1)} %compare_convert_fusion.11, s32[48]{0:T(128)S(1)} %get-tuple-element.636), kind=kOutput, calls=%fused_computation.93.clone.1 | convolution fusion | flops 151258624 | bytes 5243264 | tf_op jit(solution)/shard_map/while/body/po,pij->oij/dot_general | solution.py:41
  (128 shorter events, 85.0 us)
Async XLA Ops:
  0.0 38.4 %copy-start.1 = (s32[1,1,4]{2,1,0:T(1,128)S(1)}, s32[1,1,4]{2,1,0:T(1,128)}, u32[]{:S(2)}) copy-start(s32[1,1,4]{2,1,0:T(1,128)} %param.15) | copy-start | bytes 52
  0.0 41.6 %copy-start = (s32[1,1,4,3,192]{4,2,3,1,0:T(4,128)S(1)}, s32[1,1,4,3,192]{4,2,3,1,0:T(4,128)}, u32[]{:S(2)}) copy-start(s32[1,1,4,3,192]{4,2,3,1,0:T(4,128)} %param.14) | copy-start | bytes 27652
  1.8 12.9 %collective-permute-start = (bf16[16,128,128]{2,1,0:T(8,128)(2,1)S(1)}, bf16[16,128,128]{2,1,0:T(8,128)(2,1)S(1)}, u32[]{:S(2)}, u32[]{:S(2)}) collective-permute-start(bf16[16,128,128]{2,1,0:T(8,128)(2,1)S(1)} %bitcast_multiply_fusion), channel_id=1, source_target_pairs={{0,8},{4,12},{8,0},{12,4},{16,24},{20,28},{24,16},{28,20},{1,9},{5... | collective-permute-start | bytes 1572872 | tf_op jit(solution)/shard_map/ppermute | solution.py:10
  14.7 12.1 %collective-permute-start.1 = (bf16[16,128,128]{2,1,0:T(8,128)(2,1)S(1)}, bf16[16,128,128]{2,1,0:T(8,128)(2,1)S(1)}, u32[]{:S(2)}, u32[]{:S(2)}) collective-permute-start(bf16[16,128,128]{2,1,0:T(8,128)(2,1)S(1)} %collective-permute-done), channel_id=1, source_target_pairs={{0,1},{1,0},{2,3},{3,2},{4,5},{5,4},{6,7},{7,6},{8,9},{9,8},{10,11... | collective-permute-start | bytes 1572872 | tf_op jit(solution)/shard_map/ppermute | solution.py:10
  14.9 22.7 %collective-permute-start.4 = (bf16[16,128,128]{2,1,0:T(8,128)(2,1)S(1)}, bf16[16,128,128]{2,1,0:T(8,128)(2,1)S(1)}, u32[]{:S(2)}, u32[]{:S(2)}) collective-permute-start(bf16[16,128,128]{2,1,0:T(8,128)(2,1)S(1)} %bitcast_multiply_fusion), channel_id=1, source_target_pairs={{0,3},{1,0},{2,1},{3,2},{4,7},{5,4},{6,5},{7,6},{8,11},{9,8},{10,9... | collective-permute-start | bytes 1572872 | tf_op jit(solution)/shard_map/ppermute | solution.py:15
  28.0 10.0 %collective-permute-start.2 = (bf16[16,128,128]{2,1,0:T(8,128)(2,1)S(1)}, bf16[16,128,128]{2,1,0:T(8,128)(2,1)S(1)}, u32[]{:S(2)}, u32[]{:S(2)}) collective-permute-start(bf16[16,128,128]{2,1,0:T(8,128)(2,1)S(1)} %broadcast_select_fusion), channel_id=1, source_target_pairs={{0,16},{4,20},{8,24},{12,28},{16,0},{20,4},{24,8},{28,12},{1,17},{... | collective-permute-start | bytes 1572872 | tf_op jit(solution)/shard_map/ppermute | solution.py:10
  37.6 10.0 %collective-permute-start.6 = (bf16[16,128,128]{2,1,0:T(8,128)(2,1)S(1)}, bf16[16,128,128]{2,1,0:T(8,128)(2,1)}, u32[]{:S(2)}, u32[]{:S(2)}) collective-permute-start(bf16[16,128,128]{2,1,0:T(8,128)(2,1)S(1)} %collective-permute-done.4), channel_id=1, source_target_pairs={{0,3},{1,0},{2,1},{3,2},{4,7},{5,4},{6,5},{7,6},{8,11},{9,8},{10,9... | collective-permute-start | bytes 1572872 | tf_op jit(solution)/shard_map/ppermute | solution.py:15
  38.0 47.9 %collective-permute-start.3 = (bf16[16,128,128]{2,1,0:T(8,128)(2,1)S(1)}, bf16[16,128,128]{2,1,0:T(8,128)(2,1)S(1)}, u32[]{:S(2)}, u32[]{:S(2)}) collective-permute-start(bf16[16,128,128]{2,1,0:T(8,128)(2,1)S(1)} %collective-permute-done.2), channel_id=1, source_target_pairs={{0,2},{1,3},{2,0},{3,1},{4,6},{5,7},{6,4},{7,5},{8,10},{9,11},{10,... | collective-permute-start | bytes 1572872 | tf_op jit(solution)/shard_map/ppermute | solution.py:10
  47.6 139.1 %collective-permute-start.8 = (bf16[16,128,128]{2,1,0:T(8,128)(2,1)}, bf16[16,128,128]{2,1,0:T(8,128)(2,1)S(1)}, u32[]{:S(2)}, u32[]{:S(2)}) collective-permute-start(bf16[16,128,128]{2,1,0:T(8,128)(2,1)} %collective-permute-done.6), channel_id=1, source_target_pairs={{0,3},{1,0},{2,1},{3,2},{4,7},{5,4},{6,5},{7,6},{8,11},{9,8},{10,9... | collective-permute-start | bytes 1572872 | tf_op jit(solution)/shard_map/ppermute | solution.py:15
  86.7 33.0 %collective-permute-start.5 = (bf16[16,128,128]{2,1,0:T(8,128)(2,1)}, bf16[16,128,128]{2,1,0:T(8,128)(2,1)}, u32[]{:S(2)}, u32[]{:S(2)}) collective-permute-start(bf16[16,128,128]{2,1,0:T(8,128)(2,1)} %broadcast_select_fusion.1), channel_id=1, source_target_pairs={{0,24},{4,28},{8,0},{12,4},{16,8},{20,12},{24,16},{28,20},{1,25},{... | collective-permute-start | bytes 1572872 | tf_op jit(solution)/shard_map/ppermute | solution.py:15
  119.7 31.6 %collective-permute-start.7 = (bf16[16,128,128]{2,1,0:T(8,128)(2,1)}, bf16[16,128,128]{2,1,0:T(8,128)(2,1)}, u32[]{:S(2)}, u32[]{:S(2)}) collective-permute-start(bf16[16,128,128]{2,1,0:T(8,128)(2,1)} %collective-permute-done.5), channel_id=1, source_target_pairs={{0,24},{4,28},{8,0},{12,4},{16,8},{20,12},{24,16},{28,20},{1,25},{... | collective-permute-start | bytes 1572872 | tf_op jit(solution)/shard_map/ppermute | solution.py:15
  151.4 35.3 %collective-permute-start.9 = (bf16[16,128,128]{2,1,0:T(8,128)(2,1)}, bf16[16,128,128]{2,1,0:T(8,128)(2,1)S(1)}, u32[]{:S(2)}, u32[]{:S(2)}) collective-permute-start(bf16[16,128,128]{2,1,0:T(8,128)(2,1)} %collective-permute-done.7), channel_id=1, source_target_pairs={{0,24},{4,28},{8,0},{12,4},{16,8},{20,12},{24,16},{28,20},{1,25},{... | collective-permute-start | bytes 1572872 | tf_op jit(solution)/shard_map/ppermute | solution.py:15
where the time goes:
time: 212 us; the launch traced here: 215 us
  matrix products  112 us (53%)
  waiting for transfers between devices  74.3 us (35%)
  other arithmetic  13.7 us (6%)
  starting transfers between devices  7.74 us (4%)
  local copies, waits for them, and re-layouts  3.39 us (2%)
  between operations  2.76 us (1%)
    ppermute x4, waiting for transfers between devices, swapped_2(): lax.ppermute(value, axis, [(i, i ^ 1 << distance) for i in range(lax.axis...  60.2 us
    dot_general x16, matrix products, one_block(): jnp.einsum('po,pij->oij', out_pick, product, precision=lax.Precision.HIGH...  55.3 us
    dot_general x16, matrix products, one_block(): jnp.einsum('ps,sjk->pjk', right_pick, right_piece, preferred_element_type...  22.8 us
    dot_general x16, matrix products, one_block(): jnp.einsum('pik,pjk->pij', left_rows, right_rows, preferred_element_type=...  19.3 us
    dot_general x16, matrix products, one_block(): jnp.einsum('ps,sik->pik', left_pick, left_piece, preferred_element_type=j...  14.5 us
    ppermute x6, waiting for transfers between devices, from_behind(): lax.ppermute(value, axis, [(i, (i + by) % length) for i in range(length)])  14.2 us
    convert_element_type x16, other arithmetic, one_block(): weights = (positions < live_pairs).astype(jnp.float32)  9.86 us
    ppermute x6, starting transfers between devices, from_behind(): lax.ppermute(value, axis, [(i, (i + by) % length) for i in range(length)])  4.54 us
  transfers between devices with their start and end apart: 10, of which 5 were waited for; matrix products, arithmetic and copies ran while one was open for 46% of the time, Pallas kernels for 0%

commit v1 on v0

v1 whole, which is shorter than its diff:
```python
import functools

import jax
import jax.numpy as jnp
from jax import lax
from jax.experimental import pallas as pl
from jax.experimental.pallas import tpu as pltpu
from jax.sharding import PartitionSpec as P

SECTIONS = 4
UNROLL = 26
AXES = ("row", "col")
ROWS_BY_ROWS = (((1,), (1,)), ((), ()))


def pair_codes(pair_slots, pair_count, slots):
    pairs = pair_slots.shape[2]
    place = lax.iota(jnp.int32, pairs)
    left, right, out = pair_slots[:, 0], pair_slots[:, 1], pair_slots[:, 2]
    live = place[None, :] < pair_count[:, None]
    same = (out[:, :, None] == out[:, None, :]) & live[:, :, None] & live[:, None, :]
    rank = jnp.sum((same & (place[None, :] < place[:, None])[None]).astype(jnp.int32), axis=2)
    slot_ids = lax.iota(jnp.int32, slots)
    held = jnp.sum(((out[:, :, None] == slot_ids) & live[:, :, None]).astype(jnp.int32), axis=1)
    entries = (held + 1) // 2
    before = (out[:, :, None] > slot_ids).astype(jnp.int32)
    entry = jnp.sum(before * entries[:, None, :], axis=2) + rank // 2
    first = rank % 2 == 0
    part = jnp.where(first, (left - slots) + right * 2**12 + out * 2**24, (left - slots) * 2**6 + right * 2**18)
    room = (pairs + slots) // 2
    room = (room + UNROLL - 1) // UNROLL * UNROLL
    here = (entry[:, None, :] == lax.iota(jnp.int32, room)[None, :, None]) & live[:, None, :]
    codes = slots + slots * 2**6 + jnp.sum(jnp.where(here, part[:, None, :], 0), axis=2)
    return codes, jnp.sum(entries, axis=1)


def product_kernel(cfg, codes, meta, *refs):
    t_first, tasks, lefts, rule, has_sum = cfg
    refs = list(refs)
    left_refs = [refs[2 * s : 2 * s + 2] for s in range(lefts)]
    refs = refs[2 * lefts :]
    right_refs = [refs[4 * i : 4 * i + 4] for i in range(tasks)]
    refs = refs[4 * tasks :]
    if has_sum:
        sum_ref = refs.pop(0)
    out, left_buf, right_buf, sems = refs
    slots = out.shape[0]
    half = slots // 2
    shift, near_x, near_y = meta[SECTIONS], meta[SECTIONS + 1], meta[SECTIONS + 2]

    def section_of(i):
        return lax.rem(t_first + i + shift, SECTIONS)

    def wanted(i):
        section = section_of(i)
        if rule == "early":
            return section < SECTIONS - 1
        if rule == "late":
            return (section == SECTIONS - 1) | (i == tasks - 1)
        return section >= 0

    def copies(i):
        section = section_of(i)
        wants = wanted(i)
        found = []
        for s in range(lefts):
            for h in range(2):
                to = left_buf.at[i, pl.ds(h * half, half)]
                found.append((wants & (section == s), pltpu.make_async_copy(left_refs[s][h], to, sems.at[i, h])))
        for h, near in ((0, near_y), (1, near_x)):
            to = right_buf.at[i, pl.ds(h * half, half)]
            for k in range(2):
                found.append(
                    (wants & (near == 1 - k), pltpu.make_async_copy(right_refs[i][2 * h + k], to, sems.at[i, 2 + h]))
                )
        return found

    for i in range(tasks):
        for condition, copy in copies(i):
            pl.when(condition)(copy.start)
    if has_sum:
        sum_copy = pltpu.make_async_copy(sum_ref, out, sems.at[tasks, 0])
        sum_copy.start()
    for i in range(tasks):
        left_buf[i, slots] = jnp.zeros(left_buf.shape[2:], left_buf.dtype)
    if has_sum:
        sum_copy.wait()
    else:
        out[...] = jnp.zeros_like(out)
    for i in range(tasks):
        for condition, copy in copies(i):
            pl.when(condition)(copy.wait)

    def one_task(i, carry):
        section = section_of(i)
        blocks = jnp.where(wanted(i), (meta[section] + UNROLL - 1) // UNROLL, 0)

        def one_block(block, carry):
            products = []
            for u in range(UNROLL):
                code = codes[section, block * UNROLL + u]
                left = [left_buf[i, (code >> k) & 63] for k in (0, 6)]
                right = [right_buf[i, (code >> k) & 63] for k in (12, 18)]
                products.append(
                    lax.dot_general(
                        jnp.concatenate(left, axis=1),
                        jnp.concatenate(right, axis=1),
                        ROWS_BY_ROWS,
                        preferred_element_type=jnp.float32,
                    )
                )
            for u in range(UNROLL):
                slot = codes[section, block * UNROLL + u] >> 24
                out[slot] += products[u]
            return carry

        return lax.fori_loop(0, blocks, one_block, carry)

    lax.fori_loop(0, tasks, one_task, 0)


def add_terms(codes, meta, left, right, running, t_first, rule, slots, side):
    tasks = len(right)
    operands = [codes, meta] + [h for pair in left for h in pair] + [h for four in right for h in four]
    if running is not None:
        operands.append(running)
    work = tasks * 96 * 2 * side * side * 2 * side
    return pl.pallas_call(
        functools.partial(product_kernel, (t_first, tasks, len(left), rule, running is not None)),
        out_shape=jax.ShapeDtypeStruct((slots, side, side), jnp.float32),
        in_specs=[pl.BlockSpec(memory_space=pltpu.SMEM)] * 2 + [pl.BlockSpec(memory_space=pl.ANY)] * (len(operands) - 2),
        out_specs=pl.BlockSpec(memory_space=pltpu.VMEM),
        scratch_shapes=[
            pltpu.VMEM((tasks, slots + 1, side, side), jnp.bfloat16),
            pltpu.VMEM((tasks, slots, side, side), jnp.bfloat16),
            pltpu.SemaphoreType.DMA((tasks + 1, 4)),
        ],
        compiler_params=pltpu.CompilerParams(vmem_limit_bytes=32 * 2**20),
        cost_estimate=pl.CostEstimate(flops=2 * work, bytes_accessed=4 * 2**20, transcendentals=0),
    )(*operands)


def body(x_blocks, x_live, pair_slots, pair_count):
    row_total = lax.axis_size("row")
    col_total = lax.axis_size("col")
    layers = row_total // col_total
    panel = lax.axis_index("row") // layers
    col = lax.axis_index("col")
    slots, side = x_blocks.shape[2], x_blocks.shape[3]
    half = slots // 2

    def place(p, w, z):
        return (p * layers + w) * col_total + z

    everyone = [(p, w, z) for p in range(col_total) for w in range(layers) for z in range(col_total)]

    def moved(value, source_of):
        pairs = []
        for p, w, z in everyone:
            q, y = source_of(p, z)
            pairs.append((place(q, w, y), place(p, w, z)))
        return lax.ppermute(value, AXES, pairs)

    live = x_live[0, 0].astype(jnp.bfloat16)[:, None, None]
    first = x_blocks[0, 0, :half] * live[:half], x_blocks[0, 0, half:] * live[half:]
    codes, entries = pair_codes(pair_slots[0, 0], pair_count[0, 0], slots)

    if col_total != SECTIONS:
        filtered = jnp.concatenate(first)
        left, right = [], []
        for s in range(SECTIONS):
            a = filtered if s == 0 else moved(filtered, lambda p, z: (p, (z + s) % col_total))
            b = moved(filtered, lambda p, z: (z, (p + s) % col_total))
            left.append((a[:half], a[half:]))
            right.append((b[:half], b[:half], b[half:], b[half:]))
        meta = jnp.concatenate([entries, jnp.zeros((4,), jnp.int32)])
        return add_terms(codes, meta, left, right, None, 0, "all", slots, side)[None, None]

    near_x = panel % 2 == col % 2
    near_y = panel // 2 == col // 2
    shift = (col - panel) % SECTIONS
    meta = jnp.concatenate([entries, jnp.stack([shift, near_x.astype(jnp.int32), near_y.astype(jnp.int32), 0 * shift])])

    left = [first]
    for s in range(1, SECTIONS):
        left.append(tuple(moved(h, lambda p, z: (p, (z + 1) % col_total)) for h in left[-1]))

    def spread(t):
        a, b = left[t]
        a = jnp.where(near_x, a, moved(a, lambda p, z: (p ^ 1, z)))
        b = jnp.where(near_y, b, moved(b, lambda p, z: (p ^ 2, z)))
        return a, moved(a, lambda p, z: (p ^ 2, z)), b, moved(b, lambda p, z: (p ^ 1, z))

    right = [spread(t) for t in range(SECTIONS)]
    total = add_terms(codes, meta, left[:3], right[:2], None, 0, "early", slots, side)
    total = add_terms(codes, meta, left, right[:3], total, 0, "late", slots, side)
    total = add_terms(codes, meta, left, right[3:], total, 3, "all", slots, side)
    return total[None, None]


def solution(mesh):
    return jax.shard_map(
        body,
        mesh=mesh,
        in_specs=(
            P("row", "col", None, None, None),
            P("row", "col", None),
            P("row", "col", None, None, None),
            P("row", "col", None),
        ),
        out_specs=P("row", "col", None, None, None),
        check_vma=False,
    )
```

time: 212 us -> 71.7 us (0.34)
  the two profiles are of different devices: /device:TPU:25 before, /device:TPU:0 now
where the time goes in v1:
time: 71.7 us
  starting transfers between devices  36.4 us (51%)
  waiting for transfers between devices  22.8 us (32%)
  Pallas kernels  7.91 us (11%)
  other arithmetic  3.49 us (5%)
  local copies, waits for them, and re-layouts  0.82 us (1%)
    ppermute x22, starting transfers between devices, moved(): return lax.ppermute(value, AXES, pairs)  36.4 us
    ppermute x22, waiting for transfers between devices, moved(): return lax.ppermute(value, AXES, pairs)  22.8 us
    pallas_call x3, Pallas kernels, add_terms(): pl.pallas_call(functools.partial(product_kernel, (t_first, tasks, len(lef...  7.91 us
  transfers between devices with their start and end apart: 22, of which 8 were waited for; matrix products, arithmetic and copies ran while one was open for 2% of the time, Pallas kernels for 7%

profile of v1, /device:TPU:0, one launch (start us, length us, event | category | flops | bytes accessed | tf_op | source)
XLA Modules:
  0.0 71.7 jit_solution(10238441021501479340)
XLA Ops:
  1.9 5.1 %collective-permute-start.1 = (bf16[8,128,128]{2,1,0:T(8,128)(2,1)S(1)}, bf16[8,128,128]{2,1,0:T(8,128)(2,1)S(1)}, u32[]{:S(2)}, u32[]{:S(2)}) collective-permute-start(bf16[8,128,128]{2,1,0:T(8,128)(2,1)S(1)} %get-tuple-element.7.refs_1_), channel_id=1, source_target_pairs={{1,0},{2,1},{3,2},{0,3},{5,4},{6,5},{7,6},{4,7},{9,8},{10,9},{11,1... | collective-permute-start | bytes 786440 | tf_op jit(solution)/shard_map/ppermute | solution.py:162
  7.0 1.5 %collective-permute-start.12 = (bf16[8,128,128]{2,1,0:T(8,128)(2,1)S(1)}, bf16[8,128,128]{2,1,0:T(8,128)(2,1)S(1)}, u32[]{:S(2)}, u32[]{:S(2)}) collective-permute-start(bf16[8,128,128]{2,1,0:T(8,128)(2,1)S(1)} %get-tuple-element.7.refs_1_), channel_id=1, source_target_pairs={{16,0},{17,1},{18,2},{19,3},{20,4},{21,5},{22,6},{23,7},{24,8},{25... | collective-permute-start | bytes 786440 | tf_op jit(solution)/shard_map/ppermute | solution.py:162
  8.9 1.5 %collective-permute-start.10 = (bf16[8,128,128]{2,1,0:T(8,128)(2,1)S(1)}, bf16[8,128,128]{2,1,0:T(8,128)(2,1)S(1)}, u32[]{:S(2)}, u32[]{:S(2)}) collective-permute-start(bf16[8,128,128]{2,1,0:T(8,128)(2,1)S(1)} %get-tuple-element.8.refs_0_), channel_id=1, source_target_pairs={{8,0},{9,1},{10,2},{11,3},{12,4},{13,5},{14,6},{15,7},{0,8},{1,9},... | collective-permute-start | bytes 786440 | tf_op jit(solution)/shard_map/ppermute | solution.py:162
  13.7 1.5 %collective-permute-start.16 = (bf16[8,128,128]{2,1,0:T(8,128)(2,1)S(1)}, bf16[8,128,128]{2,1,0:T(8,128)(2,1)S(1)}, u32[]{:S(2)}, u32[]{:S(2)}) collective-permute-start(bf16[8,128,128]{2,1,0:T(8,128)(2,1)S(1)} %collective-permute-done.1.refs_3_), channel_id=1, source_target_pairs={{16,0},{17,1},{18,2},{19,3},{20,4},{21,5},{22,6},{23,7},{24,8},{25... | collective-permute-start | bytes 786440 | tf_op jit(solution)/shard_map/ppermute | solution.py:162
  15.2 4.3 %collective-permute-start.3 = (bf16[8,128,128]{2,1,0:T(8,128)(2,1)S(1)}, bf16[8,128,128]{2,1,0:T(8,128)(2,1)S(1)}, u32[]{:S(2)}, u32[]{:S(2)}) collective-permute-start(bf16[8,128,128]{2,1,0:T(8,128)(2,1)S(1)} %collective-permute-done.1.refs_3_), channel_id=1, source_target_pairs={{1,0},{2,1},{3,2},{0,3},{5,4},{6,5},{7,6},{4,7},{9,8},{10,9},{11,1... | collective-permute-start | bytes 786440 | tf_op jit(solution)/shard_map/ppermute | solution.py:162
  19.5 3.9 %collective-permute-start.2 = (bf16[8,128,128]{2,1,0:T(8,128)(2,1)S(1)}, bf16[8,128,128]{2,1,0:T(8,128)(2,1)S(1)}, u32[]{:S(2)}, u32[]{:S(2)}) collective-permute-start(bf16[8,128,128]{2,1,0:T(8,128)(2,1)S(1)} %collective-permute-done.refs_2_), channel_id=1, source_target_pairs={{1,0},{2,1},{3,2},{0,3},{5,4},{6,5},{7,6},{4,7},{9,8},{10,9},{11,1... | collective-permute-start | bytes 786440 | tf_op jit(solution)/shard_map/ppermute | solution.py:162
  23.4 1.6 %collective-permute-start.13 = (bf16[8,128,128]{2,1,0:T(8,128)(2,1)S(1)}, bf16[8,128,128]{2,1,0:T(8,128)(2,1)S(1)}, u32[]{:S(2)}, u32[]{:S(2)}) collective-permute-start(bf16[8,128,128]{2,1,0:T(8,128)(2,1)S(1)} %broadcast_select_fusion.2.refs_8_.refs_10_), channel_id=1, source_target_pairs={{8,0},{9,1},{10,2},{11,3},{12,4},{13,5},{14,6},{15,7},{0,8},{1,9},... | collective-permute-start | bytes 786440 | tf_op jit(solution)/shard_map/ppermute | solution.py:162
  25.6 1.8 %collective-permute-start.11 = (bf16[8,128,128]{2,1,0:T(8,128)(2,1)S(1)}, bf16[8,128,128]{2,1,0:T(8,128)(2,1)S(1)}, u32[]{:S(2)}, u32[]{:S(2)}) collective-permute-start(bf16[8,128,128]{2,1,0:T(8,128)(2,1)S(1)} %broadcast_select_fusion.6.refs_6_.refs_8_), channel_id=1, source_target_pairs={{16,0},{17,1},{18,2},{19,3},{20,4},{21,5},{22,6},{23,7},{24,8},{25... | collective-permute-start | bytes 786440 | tf_op jit(solution)/shard_map/ppermute | solution.py:162
  27.7 1.7 %collective-permute-done.2.refs_4_ = bf16[8,128,128]{2,1,0:T(8,128)(2,1)S(1)} collective-permute-done((bf16[8,128,128]{2,1,0:T(8,128)(2,1)S(1)}, bf16[8,128,128]{2,1,0:T(8,128)(2,1)S(1)}, u32[]{:S(2)}, u32[]{:S(2)}) %collective-permute-start.2) | collective-permute-done | bytes 262176 | tf_op jit(solution)/shard_map/ppermute | solution.py:162
  30.9 7.4 %collective-permute-done.14 = bf16[8,128,128]{2,1,0:T(8,128)(2,1)S(1)} collective-permute-done((bf16[8,128,128]{2,1,0:T(8,128)(2,1)S(1)}, bf16[8,128,128]{2,1,0:T(8,128)(2,1)S(1)}, u32[]{:S(2)}, u32[]{:S(2)}) %collective-permute-start.14) | collective-permute-done | bytes 262176 | tf_op jit(solution)/shard_map/ppermute | solution.py:162
  38.4 1.5 %collective-permute-start.17 = (bf16[8,128,128]{2,1,0:T(8,128)(2,1)S(1)}, bf16[8,128,128]{2,1,0:T(8,128)(2,1)S(1)}, u32[]{:S(2)}, u32[]{:S(2)}) collective-permute-start(bf16[8,128,128]{2,1,0:T(8,128)(2,1)S(1)} %broadcast_select_fusion.1.refs_12_.refs_14_), channel_id=1, source_target_pairs={{8,0},{9,1},{10,2},{11,3},{12,4},{13,5},{14,6},{15,7},{0,8},{1,9},... | collective-permute-start | bytes 786440 | tf_op jit(solution)/shard_map/ppermute | solution.py:162
  39.9 1.8 %collective-permute-start.15 = (bf16[8,128,128]{2,1,0:T(8,128)(2,1)S(1)}, bf16[8,128,128]{2,1,0:T(8,128)(2,1)S(1)}, u32[]{:S(2)}, u32[]{:S(2)}) collective-permute-start(bf16[8,128,128]{2,1,0:T(8,128)(2,1)S(1)} %broadcast_select_fusion.5.refs_10_.refs_12_), channel_id=1, source_target_pairs={{16,0},{17,1},{18,2},{19,3},{20,4},{21,5},{22,6},{23,7},{24,8},{25... | collective-permute-start | bytes 786440 | tf_op jit(solution)/shard_map/ppermute | solution.py:162
  41.7 2.3 %collective-permute-done.18 = bf16[8,128,128]{2,1,0:T(8,128)(2,1)S(1)} collective-permute-done((bf16[8,128,128]{2,1,0:T(8,128)(2,1)S(1)}, bf16[8,128,128]{2,1,0:T(8,128)(2,1)S(1)}, u32[]{:S(2)}, u32[]{:S(2)}) %collective-permute-start.18) | collective-permute-done | bytes 262176 | tf_op jit(solution)/shard_map/ppermute | solution.py:162
  44.1 1.6 %collective-permute-start.21 = (bf16[8,128,128]{2,1,0:T(8,128)(2,1)S(1)}, bf16[8,128,128]{2,1,0:T(8,128)(2,1)S(1)}, u32[]{:S(2)}, u32[]{:S(2)}) collective-permute-start(bf16[8,128,128]{2,1,0:T(8,128)(2,1)S(1)} %broadcast_select_fusion.refs_18_), channel_id=1, source_target_pairs={{8,0},{9,1},{10,2},{11,3},{12,4},{13,5},{14,6},{15,7},{0,8},{1,9},... | collective-permute-start | bytes 786440 | tf_op jit(solution)/shard_map/ppermute | solution.py:162
  45.6 4.0 %collective-permute-done.17.refs_13_.refs_15_ = bf16[8,128,128]{2,1,0:T(8,128)(2,1)S(1)} collective-permute-done((bf16[8,128,128]{2,1,0:T(8,128)(2,1)S(1)}, bf16[8,128,128]{2,1,0:T(8,128)(2,1)S(1)}, u32[]{:S(2)}, u32[]{:S(2)}) %collective-permute-start.17) | collective-permute-done | bytes 262176 | tf_op jit(solution)/shard_map/ppermute | solution.py:162
  49.6 1.7 %collective-permute-start.19 = (bf16[8,128,128]{2,1,0:T(8,128)(2,1)S(1)}, bf16[8,128,128]{2,1,0:T(8,128)(2,1)S(1)}, u32[]{:S(2)}, u32[]{:S(2)}) collective-permute-start(bf16[8,128,128]{2,1,0:T(8,128)(2,1)S(1)} %broadcast_select_fusion.4.refs_16_), channel_id=1, source_target_pairs={{16,0},{17,1},{18,2},{19,3},{20,4},{21,5},{22,6},{23,7},{24,8},{25... | collective-permute-start | bytes 786440 | tf_op jit(solution)/shard_map/ppermute | solution.py:162
  52.1 1.5 %collective-permute-start.6 = (bf16[8,128,128]{2,1,0:T(8,128)(2,1)S(1)}, bf16[8,128,128]{2,1,0:T(8,128)(2,1)S(1)}, u32[]{:S(2)}, u32[]{:S(2)}) collective-permute-start(bf16[8,128,128]{2,1,0:T(8,128)(2,1)S(1)} %collective-permute-done.4.refs_6_), channel_id=1, source_target_pairs={{8,0},{9,1},{10,2},{11,3},{12,4},{13,5},{14,6},{15,7},{0,8},{1,9},... | collective-permute-start | bytes 786440 | tf_op jit(solution)/shard_map/ppermute | solution.py:162
  53.6 2.3 %shard_map.46.refs_20_ = f32[16,128,128]{2,1,0:T(8,128)S(1)} custom-call(s32[4,104]{1,0:T(4,128)S(1)} %broadcast_add_fusion.codes, s32[8]{0:T(128)S(1)} %concatenate.3.meta, bf16[8,128,128]{2,1,0:T(8,128)(2,1)S(1)} %get-tuple-element.8.refs_0_, bf16[8,128,128]{2,1,0:T(8,128)(2,1)S(1)} %get-tuple-element.7.refs_1_, ...), custom_call_target="tpu_custom_call" | custom-call | flops 3221225472 | bytes 4194304 | tf_op jit(solution)/shard_map/pallas_call | solution.py:128
  55.9 4.5 %collective-permute-done.8 = bf16[8,128,128]{2,1,0:T(8,128)(2,1)S(1)} collective-permute-done((bf16[8,128,128]{2,1,0:T(8,128)(2,1)S(1)}, bf16[8,128,128]{2,1,0:T(8,128)(2,1)S(1)}, u32[]{:S(2)}, u32[]{:S(2)}) %collective-permute-start.8) | collective-permute-done | bytes 262176 | tf_op jit(solution)/shard_map/ppermute | solution.py:162
  60.5 1.6 %collective-permute-start.9 = (bf16[8,128,128]{2,1,0:T(8,128)(2,1)S(1)}, bf16[8,128,128]{2,1,0:T(8,128)(2,1)S(1)}, u32[]{:S(2)}, u32[]{:S(2)}) collective-permute-start(bf16[8,128,128]{2,1,0:T(8,128)(2,1)S(1)} %broadcast_select_fusion.3.refs_10_), channel_id=1, source_target_pairs={{8,0},{9,1},{10,2},{11,3},{12,4},{13,5},{14,6},{15,7},{0,8},{1,9},... | collective-permute-start | bytes 786440 | tf_op jit(solution)/shard_map/ppermute | solution.py:162
  62.1 2.2 %collective-permute-start.7 = (bf16[8,128,128]{2,1,0:T(8,128)(2,1)S(1)}, bf16[8,128,128]{2,1,0:T(8,128)(2,1)S(1)}, u32[]{:S(2)}, u32[]{:S(2)}) collective-permute-start(bf16[8,128,128]{2,1,0:T(8,128)(2,1)S(1)} %broadcast_select_fusion.7.refs_8_), channel_id=1, source_target_pairs={{16,0},{17,1},{18,2},{19,3},{20,4},{21,5},{22,6},{23,7},{24,8},{25... | collective-permute-start | bytes 786440 | tf_op jit(solution)/shard_map/ppermute | solution.py:162
  64.2 2.5 %shard_map.47.refs_12_ = f32[16,128,128]{2,1,0:T(8,128)S(1)} custom-call(s32[4,104]{1,0:T(4,128)S(1)} %broadcast_add_fusion.codes, s32[8]{0:T(128)S(1)} %concatenate.3.meta, bf16[8,128,128]{2,1,0:T(8,128)(2,1)S(1)} %get-tuple-element.8.refs_0_, bf16[8,128,128]{2,1,0:T(8,128)(2,1)S(1)} %get-tuple-element.7.refs_1_, ...), custom_call_target="tpu_custom_call" | custom-call | flops 4831838208 | bytes 4194304 | tf_op jit(solution)/shard_map/pallas_call | solution.py:128
  66.9 1.7 %collective-permute-done.7.refs_9_ = bf16[8,128,128]{2,1,0:T(8,128)(2,1)S(1)} collective-permute-done((bf16[8,128,128]{2,1,0:T(8,128)(2,1)S(1)}, bf16[8,128,128]{2,1,0:T(8,128)(2,1)S(1)}, u32[]{:S(2)}, u32[]{:S(2)}) %collective-permute-start.7) | collective-permute-done | bytes 262176 | tf_op jit(solution)/shard_map/ppermute | solution.py:162
  68.6 3.1 %shard_map.48 = f32[16,128,128]{2,1,0:T(8,128)} custom-call(s32[4,104]{1,0:T(4,128)S(1)} %broadcast_add_fusion.codes, s32[8]{0:T(128)S(1)} %concatenate.3.meta, bf16[8,128,128]{2,1,0:T(8,128)(2,1)S(1)} %get-tuple-element.8.refs_0_, bf16[8,128,128]{2,1,0:T(8,128)(2,1)S(1)} %get-tuple-element.7.refs_1_, bf16[8,128,128]{2,1,0:T(8,128)(2,1)S(1)} %collective-permute-done.refs_2_, ...), custom_call_target="tpu_custom_call" | custom-call | flops 1610612736 | bytes 4194304 | tf_op jit(solution)/shard_map/pallas_call | solution.py:128
  (50 shorter events, 9.0 us)
Async XLA Ops:
  1.9 11.8 %collective-permute-start.1 = (bf16[8,128,128]{2,1,0:T(8,128)(2,1)S(1)}, bf16[8,128,128]{2,1,0:T(8,128)(2,1)S(1)}, u32[]{:S(2)}, u32[]{:S(2)}) collective-permute-start(bf16[8,128,128]{2,1,0:T(8,128)(2,1)S(1)} %get-tuple-element.7.refs_1_), channel_id=1, source_target_pairs={{1,0},{2,1},{3,2},{0,3},{5,4},{6,5},{7,6},{4,7},{9,8},{10,9},{11,1... | collective-permute-start | bytes 786440 | tf_op jit(solution)/shard_map/ppermute | solution.py:162
  7.0 16.4 %collective-permute-start.12 = (bf16[8,128,128]{2,1,0:T(8,128)(2,1)S(1)}, bf16[8,128,128]{2,1,0:T(8,128)(2,1)S(1)}, u32[]{:S(2)}, u32[]{:S(2)}) collective-permute-start(bf16[8,128,128]{2,1,0:T(8,128)(2,1)S(1)} %get-tuple-element.7.refs_1_), channel_id=1, source_target_pairs={{16,0},{17,1},{18,2},{19,3},{20,4},{21,5},{22,6},{23,7},{24,8},{25... | collective-permute-start | bytes 786440 | tf_op jit(solution)/shard_map/ppermute | solution.py:162
  8.5 2.0 %copy-start = (s32[1,1,4,3,192]{4,2,3,1,0:T(4,128)S(1)}, s32[1,1,4,3,192]{4,2,3,1,0:T(4,128)}, u32[]{:S(2)}) copy-start(s32[1,1,4,3,192]{4,2,3,1,0:T(4,128)} %param.6) | copy-start | bytes 27652
  8.5 11.0 %collective-permute-start = (bf16[8,128,128]{2,1,0:T(8,128)(2,1)S(1)}, bf16[8,128,128]{2,1,0:T(8,128)(2,1)S(1)}, u32[]{:S(2)}, u32[]{:S(2)}) collective-permute-start(bf16[8,128,128]{2,1,0:T(8,128)(2,1)S(1)} %get-tuple-element.8.refs_0_), channel_id=1, source_target_pairs={{1,0},{2,1},{3,2},{0,3},{5,4},{6,5},{7,6},{4,7},{9,8},{10,9},{11,1... | collective-permute-start | bytes 786440 | tf_op jit(solution)/shard_map/ppermute | solution.py:162
  8.9 16.0 %collective-permute-start.10 = (bf16[8,128,128]{2,1,0:T(8,128)(2,1)S(1)}, bf16[8,128,128]{2,1,0:T(8,128)(2,1)S(1)}, u32[]{:S(2)}, u32[]{:S(2)}) collective-permute-start(bf16[8,128,128]{2,1,0:T(8,128)(2,1)S(1)} %get-tuple-element.8.refs_0_), channel_id=1, source_target_pairs={{8,0},{9,1},{10,2},{11,3},{12,4},{13,5},{14,6},{15,7},{0,8},{1,9},... | collective-permute-start | bytes 786440 | tf_op jit(solution)/shard_map/ppermute | solution.py:162
  10.5 0.7 copy-start.1
  13.7 11.9 %collective-permute-start.16 = (bf16[8,128,128]{2,1,0:T(8,128)(2,1)S(1)}, bf16[8,128,128]{2,1,0:T(8,128)(2,1)S(1)}, u32[]{:S(2)}, u32[]{:S(2)}) collective-permute-start(bf16[8,128,128]{2,1,0:T(8,128)(2,1)S(1)} %collective-permute-done.1.refs_3_), channel_id=1, source_target_pairs={{16,0},{17,1},{18,2},{19,3},{20,4},{21,5},{22,6},{23,7},{24,8},{25... | collective-permute-start | bytes 786440 | tf_op jit(solution)/shard_map/ppermute | solution.py:162
  15.2 12.1 %collective-permute-start.3 = (bf16[8,128,128]{2,1,0:T(8,128)(2,1)S(1)}, bf16[8,128,128]{2,1,0:T(8,128)(2,1)S(1)}, u32[]{:S(2)}, u32[]{:S(2)}) collective-permute-start(bf16[8,128,128]{2,1,0:T(8,128)(2,1)S(1)} %collective-permute-done.1.refs_3_), channel_id=1, source_target_pairs={{1,0},{2,1},{3,2},{0,3},{5,4},{6,5},{7,6},{4,7},{9,8},{10,9},{11,1... | collective-permute-start | bytes 786440 | tf_op jit(solution)/shard_map/ppermute | solution.py:162
  19.5 9.9 %collective-permute-start.2 = (bf16[8,128,128]{2,1,0:T(8,128)(2,1)S(1)}, bf16[8,128,128]{2,1,0:T(8,128)(2,1)S(1)}, u32[]{:S(2)}, u32[]{:S(2)}) collective-permute-start(bf16[8,128,128]{2,1,0:T(8,128)(2,1)S(1)} %collective-permute-done.refs_2_), channel_id=1, source_target_pairs={{1,0},{2,1},{3,2},{0,3},{5,4},{6,5},{7,6},{4,7},{9,8},{10,9},{11,1... | collective-permute-start | bytes 786440 | tf_op jit(solution)/shard_map/ppermute | solution.py:162
  23.4 16.5 %collective-permute-start.13 = (bf16[8,128,128]{2,1,0:T(8,128)(2,1)S(1)}, bf16[8,128,128]{2,1,0:T(8,128)(2,1)S(1)}, u32[]{:S(2)}, u32[]{:S(2)}) collective-permute-start(bf16[8,128,128]{2,1,0:T(8,128)(2,1)S(1)} %broadcast_select_fusion.2.refs_8_.refs_10_), channel_id=1, source_target_pairs={{8,0},{9,1},{10,2},{11,3},{12,4},{13,5},{14,6},{15,7},{0,8},{1,9},... | collective-permute-start | bytes 786440 | tf_op jit(solution)/shard_map/ppermute | solution.py:162
  25.0 13.4 %collective-permute-start.14 = (bf16[8,128,128]{2,1,0:T(8,128)(2,1)S(1)}, bf16[8,128,128]{2,1,0:T(8,128)(2,1)S(1)}, u32[]{:S(2)}, u32[]{:S(2)}) collective-permute-start(bf16[8,128,128]{2,1,0:T(8,128)(2,1)S(1)} %collective-permute-done.refs_2_), channel_id=1, source_target_pairs={{8,0},{9,1},{10,2},{11,3},{12,4},{13,5},{14,6},{15,7},{0,8},{1,9},... | collective-permute-start | bytes 786440 | tf_op jit(solution)/shard_map/ppermute | solution.py:162
  25.6 18.5 %collective-permute-start.11 = (bf16[8,128,128]{2,1,0:T(8,128)(2,1)S(1)}, bf16[8,128,128]{2,1,0:T(8,128)(2,1)S(1)}, u32[]{:S(2)}, u32[]{:S(2)}) collective-permute-start(bf16[8,128,128]{2,1,0:T(8,128)(2,1)S(1)} %broadcast_select_fusion.6.refs_6_.refs_8_), channel_id=1, source_target_pairs={{16,0},{17,1},{18,2},{19,3},{20,4},{21,5},{22,6},{23,7},{24,8},{25... | collective-permute-start | bytes 786440 | tf_op jit(solution)/shard_map/ppermute | solution.py:162
  27.4 14.3 %collective-permute-start.20 = (bf16[8,128,128]{2,1,0:T(8,128)(2,1)S(1)}, bf16[8,128,128]{2,1,0:T(8,128)(2,1)S(1)}, u32[]{:S(2)}, u32[]{:S(2)}) collective-permute-start(bf16[8,128,128]{2,1,0:T(8,128)(2,1)S(1)} %collective-permute-done.3.refs_5_), channel_id=1, source_target_pairs={{16,0},{17,1},{18,2},{19,3},{20,4},{21,5},{22,6},{23,7},{24,8},{25... | collective-permute-start | bytes 786440 | tf_op jit(solution)/shard_map/ppermute | solution.py:162
  29.4 14.6 %collective-permute-start.18 = (bf16[8,128,128]{2,1,0:T(8,128)(2,1)S(1)}, bf16[8,128,128]{2,1,0:T(8,128)(2,1)S(1)}, u32[]{:S(2)}, u32[]{:S(2)}) collective-permute-start(bf16[8,128,128]{2,1,0:T(8,128)(2,1)S(1)} %collective-permute-done.2.refs_4_), channel_id=1, source_target_pairs={{8,0},{9,1},{10,2},{11,3},{12,4},{13,5},{14,6},{15,7},{0,8},{1,9},... | collective-permute-start | bytes 786440 | tf_op jit(solution)/shard_map/ppermute | solution.py:162
  38.4 11.2 %collective-permute-start.17 = (bf16[8,128,128]{2,1,0:T(8,128)(2,1)S(1)}, bf16[8,128,128]{2,1,0:T(8,128)(2,1)S(1)}, u32[]{:S(2)}, u32[]{:S(2)}) collective-permute-start(bf16[8,128,128]{2,1,0:T(8,128)(2,1)S(1)} %broadcast_select_fusion.1.refs_12_.refs_14_), channel_id=1, source_target_pairs={{8,0},{9,1},{10,2},{11,3},{12,4},{13,5},{14,6},{15,7},{0,8},{1,9},... | collective-permute-start | bytes 786440 | tf_op jit(solution)/shard_map/ppermute | solution.py:162
  39.9 13.7 %collective-permute-start.15 = (bf16[8,128,128]{2,1,0:T(8,128)(2,1)S(1)}, bf16[8,128,128]{2,1,0:T(8,128)(2,1)S(1)}, u32[]{:S(2)}, u32[]{:S(2)}) collective-permute-start(bf16[8,128,128]{2,1,0:T(8,128)(2,1)S(1)} %broadcast_select_fusion.5.refs_10_.refs_12_), channel_id=1, source_target_pairs={{16,0},{17,1},{18,2},{19,3},{20,4},{21,5},{22,6},{23,7},{24,8},{25... | collective-permute-start | bytes 786440 | tf_op jit(solution)/shard_map/ppermute | solution.py:162
  41.7 10.4 %collective-permute-start.4 = (bf16[8,128,128]{2,1,0:T(8,128)(2,1)S(1)}, bf16[8,128,128]{2,1,0:T(8,128)(2,1)S(1)}, u32[]{:S(2)}, u32[]{:S(2)}) collective-permute-start(bf16[8,128,128]{2,1,0:T(8,128)(2,1)S(1)} %collective-permute-done.2.refs_4_), channel_id=1, source_target_pairs={{1,0},{2,1},{3,2},{0,3},{5,4},{6,5},{7,6},{4,7},{9,8},{10,9},{11,1... | collective-permute-start | bytes 786440 | tf_op jit(solution)/shard_map/ppermute | solution.py:162
  44.0 7.3 %collective-permute-start.5 = (bf16[8,128,128]{2,1,0:T(8,128)(2,1)S(1)}, bf16[8,128,128]{2,1,0:T(8,128)(2,1)S(1)}, u32[]{:S(2)}, u32[]{:S(2)}) collective-permute-start(bf16[8,128,128]{2,1,0:T(8,128)(2,1)S(1)} %collective-permute-done.3.refs_5_), channel_id=1, source_target_pairs={{1,0},{2,1},{3,2},{0,3},{5,4},{6,5},{7,6},{4,7},{9,8},{10,9},{11,1... | collective-permute-start | bytes 786440 | tf_op jit(solution)/shard_map/ppermute | solution.py:162
  44.1 20.2 %collective-permute-start.21 = (bf16[8,128,128]{2,1,0:T(8,128)(2,1)S(1)}, bf16[8,128,128]{2,1,0:T(8,128)(2,1)S(1)}, u32[]{:S(2)}, u32[]{:S(2)}) collective-permute-start(bf16[8,128,128]{2,1,0:T(8,128)(2,1)S(1)} %broadcast_select_fusion.refs_18_), channel_id=1, source_target_pairs={{8,0},{9,1},{10,2},{11,3},{12,4},{13,5},{14,6},{15,7},{0,8},{1,9},... | collective-permute-start | bytes 786440 | tf_op jit(solution)/shard_map/ppermute | solution.py:162
  49.6 14.7 %collective-permute-start.19 = (bf16[8,128,128]{2,1,0:T(8,128)(2,1)S(1)}, bf16[8,128,128]{2,1,0:T(8,128)(2,1)S(1)}, u32[]{:S(2)}, u32[]{:S(2)}) collective-permute-start(bf16[8,128,128]{2,1,0:T(8,128)(2,1)S(1)} %broadcast_select_fusion.4.refs_16_), channel_id=1, source_target_pairs={{16,0},{17,1},{18,2},{19,3},{20,4},{21,5},{22,6},{23,7},{24,8},{25... | collective-permute-start | bytes 786440 | tf_op jit(solution)/shard_map/ppermute | solution.py:162
  51.3 9.1 %collective-permute-start.8 = (bf16[8,128,128]{2,1,0:T(8,128)(2,1)S(1)}, bf16[8,128,128]{2,1,0:T(8,128)(2,1)S(1)}, u32[]{:S(2)}, u32[]{:S(2)}) collective-permute-start(bf16[8,128,128]{2,1,0:T(8,128)(2,1)S(1)} %collective-permute-done.5.refs_7_), channel_id=1, source_target_pairs={{16,0},{17,1},{18,2},{19,3},{20,4},{21,5},{22,6},{23,7},{24,8},{25... | collective-permute-start | bytes 786440 | tf_op jit(solution)/shard_map/ppermute | solution.py:162
  52.1 10.0 %collective-permute-start.6 = (bf16[8,128,128]{2,1,0:T(8,128)(2,1)S(1)}, bf16[8,128,128]{2,1,0:T(8,128)(2,1)S(1)}, u32[]{:S(2)}, u32[]{:S(2)}) collective-permute-start(bf16[8,128,128]{2,1,0:T(8,128)(2,1)S(1)} %collective-permute-done.4.refs_6_), channel_id=1, source_target_pairs={{8,0},{9,1},{10,2},{11,3},{12,4},{13,5},{14,6},{15,7},{0,8},{1,9},... | collective-permute-start | bytes 786440 | tf_op jit(solution)/shard_map/ppermute | solution.py:162
  60.5 6.4 %collective-permute-start.9 = (bf16[8,128,128]{2,1,0:T(8,128)(2,1)S(1)}, bf16[8,128,128]{2,1,0:T(8,128)(2,1)S(1)}, u32[]{:S(2)}, u32[]{:S(2)}) collective-permute-start(bf16[8,128,128]{2,1,0:T(8,128)(2,1)S(1)} %broadcast_select_fusion.3.refs_10_), channel_id=1, source_target_pairs={{8,0},{9,1},{10,2},{11,3},{12,4},{13,5},{14,6},{15,7},{0,8},{1,9},... | collective-permute-start | bytes 786440 | tf_op jit(solution)/shard_map/ppermute | solution.py:162
  62.1 6.5 %collective-permute-start.7 = (bf16[8,128,128]{2,1,0:T(8,128)(2,1)S(1)}, bf16[8,128,128]{2,1,0:T(8,128)(2,1)S(1)}, u32[]{:S(2)}, u32[]{:S(2)}) collective-permute-start(bf16[8,128,128]{2,1,0:T(8,128)(2,1)S(1)} %broadcast_select_fusion.7.refs_8_), channel_id=1, source_target_pairs={{16,0},{17,1},{18,2},{19,3},{20,4},{21,5},{22,6},{23,7},{24,8},{25... | collective-permute-start | bytes 786440 | tf_op jit(solution)/shard_map/ppermute | solution.py:162
